TPU v7x, 512 devices: a whole 4x8x8 slice. The times are simulated.
512 devices in a mesh: sweep: 8 (over z_lo, core), recv: 64 (over x, y, z_hi).
Axes of the slice: x: 4, y: 8, z: 8 (z_hi: 2, z_lo: 4; z = z_hi * 4 + z_lo), core: 2. Of those that a mesh axis runs over, the one named last changes fastest.
Arguments:
- records: bfloat16 [16, 4096, 4096], P('sweep', 'recv'), may hold values from -6 to 6
- pilots: bfloat16 [16, 3968], replicated, may hold values from -0.09375 to 0.09375
- hadamard: int32 [16, 16], replicated, may hold values from -1 to 1, as said below
- code_vibrator: int32 [16], replicated, may hold values from 0 to 15, each once
- owner_map: int32 [4096], P('recv'), may hold values from 0 to 15
- live_mask: int32 [4096], P('recv'), may hold values 0 or 1
- filters: bfloat16 [16, 128, 128], P('sweep'), may hold values from -0.5 to 0.5
- targets: bfloat16 [16, 4096, 128], P('sweep', 'recv'), may hold values from -6 to 6
Outputs:
- responses: float32 [16, 4096, 128], P('sweep', 'recv')
- gradient: float32 [16, 128, 128], P('sweep', 'recv')
Inputs may be any that keep to these rules, and one draw needn't show every extreme that they name: hadamard transposed times hadamard is 16 times the identity. `code_vibrator`: every vibrator belongs to exactly one code.
All inputs are finite; a program needn't handle non-finite values. No bound on the sum of `live_mask` on one device may be relied on, other than what follows from the above.
Results may differ from a plain program's by a relative error of at most 0.0085.
Values may be sent and summed in bfloat16 or wider, within the bound.
A program may use at most 64 MiB of HBM per device.

v0:
```python
import math
import jax
import jax.numpy as jnp
from jax import lax
from jax.sharding import PartitionSpec as P


def toeplitz(sweep_pilot, samples, lagcount):
    padding = jnp.zeros((samples + 1 - sweep_pilot.shape[0],), sweep_pilot.dtype)
    extended = jnp.concatenate([sweep_pilot, padding])
    return jnp.tile(extended, lagcount)[: lagcount * samples].reshape(lagcount, samples)


def correlate_split(combined, sweep_pilot, samples, lagcount):
    upper = combined.astype(jnp.bfloat16)
    lower = (combined - upper.astype(jnp.float32)).astype(jnp.bfloat16)
    paired = jnp.concatenate([upper, lower], axis=0)
    toe_rows = toeplitz(sweep_pilot, samples, lagcount)
    lagged = lax.dot_general(
        paired, toe_rows, (((1,), (1,)), ((), ())), preferred_element_type=jnp.float32
    )
    half = combined.shape[0]
    return lagged[:half] + lagged[half:]


def local(records, pilots, hadamard, code_vibrator, owner_map, live_mask, filters, targets):
    codes = hadamard.shape[1]
    held_sweeps = records.shape[0]
    channels = records.shape[1]
    samples = records.shape[2]
    lagcount = filters.shape[1]
    owned_codes = filters.shape[0]
    first_code = lax.axis_index("sweep") * owned_codes
    code_norm = 1.0 / math.sqrt(codes)
    onehot = (code_vibrator[:, None] == jnp.arange(codes, dtype=jnp.int32)[None, :]).astype(
        jnp.bfloat16
    )
    code_pilot = jnp.dot(onehot, pilots, preferred_element_type=jnp.float32).astype(jnp.bfloat16)
    sign_table = hadamard.astype(jnp.bfloat16)
    sign_rows = lax.dynamic_slice_in_dim(
        sign_table, lax.axis_index("sweep") * held_sweeps, held_sweeps, 0
    )

    def column(operands):
        sweep_pilot, signs_col = operands
        combined = jnp.einsum("s,srt->rt", signs_col, records, preferred_element_type=jnp.float32)
        return code_norm * correlate_split(combined, sweep_pilot, samples, lagcount)

    decoded = lax.psum_scatter(
        lax.map(column, (code_pilot, sign_rows.T)), "sweep", scatter_dimension=0, tiled=True
    ).astype(jnp.bfloat16)
    col_vibs = lax.dynamic_slice_in_dim(code_vibrator, first_code, owned_codes, 0)
    responses = jnp.einsum("crl,clm->crm", decoded, filters, preferred_element_type=jnp.float32)
    owned = (owner_map[None, :] == col_vibs[:, None]).astype(jnp.float32)
    weight = live_mask.astype(jnp.float32)[None, :] * (0.25 + owned)
    residual = (weight[:, :, None] * (responses - targets.astype(jnp.float32))).astype(jnp.bfloat16)
    factor = 1.0 / math.sqrt(channels * lax.axis_size("recv"))
    local_grad = (
        jnp.einsum("crl,crm->clm", decoded, residual, preferred_element_type=jnp.float32) * factor
    )
    summed = lax.psum(local_grad, "recv")
    share_rows = lagcount // lax.axis_size("recv")
    gradient = lax.dynamic_slice_in_dim(summed, lax.axis_index("recv") * share_rows, share_rows, 1)
    return (responses, gradient)


def solution(mesh):
    in_specs = (
        P("sweep", "recv", None),
        P(),
        P(),
        P(),
        P("recv"),
        P("recv"),
        P("sweep", None, None),
        P("sweep", "recv", None),
    )
    out_specs = (P("sweep", "recv", None), P("sweep", "recv", None))
    return jax.shard_map(local, mesh=mesh, in_specs=in_specs, out_specs=out_specs, check_vma=False)
```

profile of v0, /device:TPU:8, one launch (start us, length us, event | category | flops | bytes accessed | tf_op | source)
XLA Modules:
  0.0 939.9 jit_solution(15561842590453519801)
XLA Ops:
  8.1 0.9 convolution_convert_fusion
  9.0 97.8 %while.10 = (s32[]{:T(128)}, f32[16,64,128]{2,1,0:T(8,128)}, bf16[16,2]{1,0:T(8,128)(2,1)S(1)}, bf16[2,64,4096]{2,1,0:T(8,128)(2,1)}, bf16[16,3968]{1,0:T(8,128)(2,1)S(1)}, /*index=5*/s32[]{:T(128)}, bf16[]{:T(256)}) while((s32[]{:T(128)}, f32[16,64,128]{2,1,0:T(8,128)}, bf16[16,2]{1,0:T(8,128)(2,1)S(1)}, bf16[2,64,4096]{2,1,0:T(8,128)(2,1)}, ...), condition=%wide.region_1.2_spmd, body=%wide.region_0.1_spmd.sunk | while | flops 138428416 | bytes 19079812 | solution.py:50
  9.2 1.1 tile.12
  10.9 0.7 copy-done.6
  11.6 1.3 fusion.35
  15.3 1.1 tile.12
  17.0 0.7 copy-done.6
  17.8 1.3 fusion.35
  21.4 1.1 tile.12
  23.2 0.7 copy-done.6
  23.9 1.3 fusion.35
  27.5 1.1 tile.12
  29.3 0.7 copy-done.6
  30.0 1.3 fusion.35
  33.6 1.1 tile.12
  35.4 0.7 copy-done.6
  36.1 1.3 fusion.35
  39.8 1.1 tile.12
  42.2 1.3 fusion.35
  45.9 1.1 tile.12
  47.6 0.7 copy-done.6
  48.3 1.3 fusion.35
  52.0 1.1 tile.12
  53.7 0.7 copy-done.6
  54.4 1.3 fusion.35
  58.1 1.1 tile.12
  59.8 0.7 copy-done.6
  60.6 1.3 fusion.35
  64.2 1.1 tile.12
  66.7 1.3 fusion.35
  70.3 1.1 tile.12
  72.8 1.3 fusion.35
  76.5 1.1 tile.12
  78.9 1.3 fusion.35
  82.6 1.1 tile.12
  85.0 1.3 fusion.35
  88.7 1.1 tile.12
  91.1 1.3 fusion.35
  94.8 1.1 tile.12
  96.5 0.7 copy-done.6
  97.2 1.3 fusion.35
  100.9 1.1 tile.12
  103.4 1.3 fusion.35
  107.1 43.9 %reduce-scatter.2.cloned.1.call-done = f32[2,64,128]{2,1,0:T(8,128)} async-done(((f32[16,64,128]{2,1,0:T(8,128)}), f32[2,64,128]{2,1,0:T(8,128)}) %reduce-scatter.2.cloned.1.call-update) | async-done | bytes 65552 | tf_op jit(solution)/shard_map/reduce_scatter | solution.py:49
  151.0 1.0 fusion.15
  152.0 1.8 convolution_multiply_fusion
  153.8 778.0 %all-reduce.3.cloned.1.call-done = f32[2,128,128]{2,1,0:T(8,128)} async-done(((f32[2,128,128]{2,1,0:T(8,128)}), f32[2,128,128]{2,1,0:T(8,128)}) %all-reduce.3.cloned.1.call-update) | async-done | bytes 131088 | tf_op jit(solution)/shard_map/psum | solution.py:61
  931.8 1.3 constant_dynamic-slice_fusion.1
  (192 shorter events, 53.0 us)
Async XLA Ops:
  7.2 0.9 copy-start
  7.2 143.8 %reduce-scatter.2.cloned.1.call-start = ((), (), s32[]{:S(2)}) async-start(), calls=%async_computation.1 | async-start | bytes 589824 | tf_op jit(solution)/shard_map/reduce_scatter | solution.py:49
  9.0 98.0 %copy-start.4 = (s32[16]{0:T(128)S(1)}, s32[16]{0:T(128)}, u32[]{:S(2)}) copy-start(s32[16]{0:T(128)} %param.13) | copy-start | bytes 196
  9.0 98.1 %copy-start.7 = (s32[64]{0:T(128)S(1)}, s32[64]{0:T(128)}, u32[]{:S(2)}) copy-start(s32[64]{0:T(128)} %param.15) | copy-start | bytes 772
  9.0 98.1 %copy-start.5 = (s32[64]{0:T(128)S(1)}, s32[64]{0:T(128)}, u32[]{:S(2)}) copy-start(s32[64]{0:T(128)} %param.14) | copy-start | bytes 772
  9.0 142.0 %copy-start.2 = (bf16[2,128,128]{2,1,0:T(8,128)(2,1)S(1)}, bf16[2,128,128]{2,1,0:T(8,128)(2,1)}, u32[]{:S(2)}) copy-start(bf16[2,128,128]{2,1,0:T(8,128)(2,1)} %param.16) | copy-start | bytes 196612
  9.0 143.0 %copy-start.3 = (bf16[2,64,128]{2,1,0:T(8,128)(2,1)S(1)}, bf16[2,64,128]{2,1,0:T(8,128)(2,1)}, u32[]{:S(2)}) copy-start(bf16[2,64,128]{2,1,0:T(8,128)(2,1)} %param.17) | copy-start | bytes 98308
  10.4 1.2 copy-start.6
  16.5 1.2 copy-start.6
  22.6 1.2 copy-start.6
  28.8 1.2 copy-start.6
  34.9 1.2 copy-start.6
  41.0 1.2 copy-start.6
  47.1 1.2 copy-start.6
  53.2 1.2 copy-start.6
  59.3 1.2 copy-start.6
  65.4 1.2 copy-start.6
  71.6 1.2 copy-start.6
  77.7 1.2 copy-start.6
  83.8 1.2 copy-start.6
  89.9 1.2 copy-start.6
  96.0 1.2 copy-start.6
  102.1 1.2 copy-start.6
  106.9 824.9 %all-reduce.3.cloned.1.call-start = ((), (), s32[]{:S(2)}) async-start(), calls=%async_computation.2 | async-start | bytes 262144 | tf_op jit(solution)/shard_map/psum | solution.py:61
  152.0 781.1 %copy-start.1 = (f32[2,64,128]{2,1,0:T(8,128)}, f32[2,64,128]{2,1,0:T(8,128)S(1)}, u32[]{:S(2)}) copy-start(f32[2,64,128]{2,1,0:T(8,128)S(1)} %fusion.15) | copy-start | bytes 196612
Sparse Core Ops, SparseCore 0:
  107.0 43.9 reduce-scatter.1
  154.2 777.6 all-reduce.2
where the time goes:
time: 941 us; the launch traced here: 940 us
  waiting for transfers between devices  822 us (87%)
  local copies, waits for them, and re-layouts  52.6 us (6%)
  matrix products  30.8 us (3%)
  other arithmetic  19.3 us (2%)
  between operations  14.1 us (1%)
    psum x1, waiting for transfers between devices, local(): summed = lax.psum(local_grad, 'recv')  778 us
    reduce_scatter x1, waiting for transfers between devices, local(): lax.psum_scatter(lax.map(column, (code_pilot, sign_rows.T)), 'sweep', sca...  43.9 us
    dot_general x16, matrix products, column(): jnp.einsum('s,srt->rt', signs_col, records, preferred_element_type=jnp.fl...  20.2 us
    another operation x32, local copies, waits for them, and re-layouts, toeplitz(): jnp.tile(extended, lagcount)[:lagcount * samples].reshape(lagcount, samples)  19.6 us
  transfers between devices with their start and end apart: 2, of which 2 were waited for; matrix products, arithmetic and copies ran while one was open for 0% of the time, Pallas kernels for 0%

commit v1 on v0

--- a/solution.py
+++ b/solution.py
@@ -58,7 +58,7 @@
     local_grad = (
         jnp.einsum("crl,crm->clm", decoded, residual, preferred_element_type=jnp.float32) * factor
     )
-    summed = lax.psum(local_grad, "recv")
+    summed = jnp.sum(lax.all_gather(local_grad, "recv"), axis=0)
     share_rows = lagcount // lax.axis_size("recv")
     gradient = lax.dynamic_slice_in_dim(summed, lax.axis_index("recv") * share_rows, share_rows, 1)
     return (responses, gradient)

time: 941 us -> 375 us (0.40)
  the two profiles are of different devices: /device:TPU:8 before, /device:TPU:2 now
where the time goes in v1:
time: 375 us; the launch traced here: 374 us
  waiting for transfers between devices  245 us (65%)
  matrix products  50.3 us (13%)
  local copies, waits for them, and re-layouts  40.4 us (11%)
  other arithmetic  22.9 us (6%)
  between operations  14.1 us (4%)
    all_gather x1, waiting for transfers between devices, local(): summed = jnp.sum(lax.all_gather(local_grad, 'recv'), axis=0)  202 us
    reduce_scatter x1, waiting for transfers between devices, local(): lax.psum_scatter(lax.map(column, (code_pilot, sign_rows.T)), 'sweep', sca...  43.9 us
    dot_general x16, matrix products, column(): jnp.einsum('s,srt->rt', signs_col, records, preferred_element_type=jnp.fl...  39.8 us
    another operation x32, local copies, waits for them, and re-layouts, toeplitz(): jnp.tile(extended, lagcount)[:lagcount * samples].reshape(lagcount, samples)  19.6 us
    dynamic_update_slice x16, other arithmetic, local(): lax.map(column, (code_pilot, sign_rows.T))  9.82 us
    convert_element_type x16, other arithmetic, correlate_split(): lower = (combined - upper.astype(jnp.float32)).astype(jnp.bfloat16)  9.22 us
    dot_general x16, local copies, waits for them, and re-layouts, column(): jnp.einsum('s,srt->rt', signs_col, records, preferred_element_type=jnp.fl...  9.18 us
    reshape x16, local copies, waits for them, and re-layouts, toeplitz(): jnp.tile(extended, lagcount)[:lagcount * samples].reshape(lagcount, samples)  7.9 us
  transfers between devices with their start and end apart: 2, of which 2 were waited for; matrix products, arithmetic and copies ran while one was open for 0% of the time, Pallas kernels for 0%

profile of v1, /device:TPU:2, one launch (start us, length us, event | category | flops | bytes accessed | tf_op | source)
XLA Modules:
  0.0 374.3 jit_solution(11026480520958797524)
XLA Ops:
  7.2 0.7 constant_dynamic-slice_fusion.2
  8.1 0.9 convolution_convert_fusion
  9.0 105.6 %while.10 = (s32[]{:T(128)}, f32[16,64,128]{2,1,0:T(8,128)}, bf16[16,2]{1,0:T(8,128)(2,1)S(1)}, bf16[2,64,4096]{2,1,0:T(8,128)(2,1)}, bf16[16,3968]{1,0:T(8,128)(2,1)S(1)}, /*index=5*/s32[]{:T(128)}, bf16[]{:T(256)}) while((s32[]{:T(128)}, f32[16,64,128]{2,1,0:T(8,128)}, bf16[16,2]{1,0:T(8,128)(2,1)S(1)}, bf16[2,64,4096]{2,1,0:T(8,128)(2,1)}, ...), condition=%wide.region_1.2_spmd, body=%wide.region_0.1_spmd.sunk | while | flops 138428416 | bytes 14885479 | solution.py:50
  9.1 2.5 fusion.35
  12.8 1.1 tile.12
  15.0 0.6 fusion.38
  15.7 2.5 fusion.35
  19.4 1.1 tile.12
  22.3 2.5 fusion.35
  26.0 1.1 tile.12
  28.2 0.6 fusion.38
  28.9 2.5 fusion.35
  32.6 1.1 tile.12
  35.5 2.5 fusion.35
  39.2 1.1 tile.12
  41.4 0.6 fusion.38
  42.1 2.5 fusion.35
  45.8 1.1 tile.12
  48.7 2.5 fusion.35
  52.4 1.1 tile.12
  54.6 0.6 fusion.38
  55.3 2.5 fusion.35
  59.0 1.1 tile.12
  61.2 0.6 fusion.38
  61.9 2.5 fusion.35
  65.6 1.1 tile.12
  67.8 0.6 fusion.38
  68.5 2.5 fusion.35
  72.2 1.1 tile.12
  75.1 2.5 fusion.35
  78.8 1.1 tile.12
  81.7 2.5 fusion.35
  85.4 1.1 tile.12
  88.3 2.5 fusion.35
  92.0 1.1 tile.12
  94.9 2.5 fusion.35
  98.6 1.1 tile.12
  100.8 0.6 fusion.38
  101.5 2.5 fusion.35
  105.2 1.1 tile.12
  107.4 0.6 fusion.38
  108.1 2.5 fusion.35
  111.8 1.1 tile.12
  114.8 43.9 %reduce-scatter.2.cloned.1.call-done = f32[2,64,128]{2,1,0:T(8,128)} async-done(((f32[16,64,128]{2,1,0:T(8,128)}), f32[2,64,128]{2,1,0:T(8,128)}) %reduce-scatter.2.cloned.1.call-update) | async-done | bytes 65552 | tf_op jit(solution)/shard_map/reduce_scatter | solution.py:49
  158.7 1.0 fusion.15
  159.7 1.7 convolution_multiply_fusion
  161.5 201.5 %all-gather.3.cloned.1.call-done = f32[128,128,128]{2,1,0:T(8,128)} async-done(((f32[2,128,128]{2,1,0:T(8,128)}), f32[128,128,128]{2,1,0:T(8,128)}) %all-gather.3.cloned.1.call-update) | async-done | bytes 8388624 | tf_op jit(solution)/shard_map/all_gather | solution.py:61
  363.0 3.8 %reduce_sum.9 = f32[2,128,128]{2,1,0:T(8,128)S(1)} reduce(f32[64,2,128,128]{3,2,1,0:T(8,128)} %bitcast.34, f32[]{:T(128)} %constant.8.clone.1), dimensions={0}, to_apply=%region_3.4 | reduce | flops 2064384 | bytes 8519684 | tf_op jit(solution)/shard_map/reduce_sum | solution.py:61
  (161 shorter events, 42.6 us)
Async XLA Ops:
  7.2 0.9 copy-start
  7.2 151.5 %reduce-scatter.2.cloned.1.call-start = ((), (), s32[]{:S(2)}) async-start(), calls=%async_computation.1 | async-start | bytes 589824 | tf_op jit(solution)/shard_map/reduce_scatter | solution.py:49
  9.0 105.7 %copy-start.4 = (s32[16]{0:T(128)S(1)}, s32[16]{0:T(128)}, u32[]{:S(2)}) copy-start(s32[16]{0:T(128)} %param.13) | copy-start | bytes 196
  9.0 105.8 %copy-start.6 = (s32[64]{0:T(128)S(1)}, s32[64]{0:T(128)}, u32[]{:S(2)}) copy-start(s32[64]{0:T(128)} %param.15) | copy-start | bytes 772
  9.0 105.8 %copy-start.5 = (s32[64]{0:T(128)S(1)}, s32[64]{0:T(128)}, u32[]{:S(2)}) copy-start(s32[64]{0:T(128)} %param.14) | copy-start | bytes 772
  9.0 149.7 %copy-start.2 = (bf16[2,128,128]{2,1,0:T(8,128)(2,1)S(1)}, bf16[2,128,128]{2,1,0:T(8,128)(2,1)}, u32[]{:S(2)}) copy-start(bf16[2,128,128]{2,1,0:T(8,128)(2,1)} %param.16) | copy-start | bytes 196612
  9.0 150.7 %copy-start.3 = (bf16[2,64,128]{2,1,0:T(8,128)(2,1)S(1)}, bf16[2,64,128]{2,1,0:T(8,128)(2,1)}, u32[]{:S(2)}) copy-start(bf16[2,64,128]{2,1,0:T(8,128)(2,1)} %param.17) | copy-start | bytes 98308
  114.6 248.4 %all-gather.3.cloned.1.call-start = ((), (), s32[]{:S(2)}) async-start(), calls=%async_computation.2 | async-start | bytes 8519680 | tf_op jit(solution)/shard_map/all_gather | solution.py:61
  159.7 207.1 %copy-start.1 = (f32[2,64,128]{2,1,0:T(8,128)}, f32[2,64,128]{2,1,0:T(8,128)S(1)}, u32[]{:S(2)}) copy-start(f32[2,64,128]{2,1,0:T(8,128)S(1)} %fusion.15) | copy-start | bytes 196612
Sparse Core Ops, SparseCore 0:
  114.7 43.9 reduce-scatter.1
  164.0 198.9 all-gather.2
